TPU v7x, 512 devices: a whole 4x4x16 slice. The times are simulated.
512 devices in a mesh: dp: 32 (over y, x, z_hi), tensor: 16 (over z_lo, core).
Axes of the slice: x: 4, y: 4, z: 16 (z_hi: 2, z_lo: 8; z = z_hi * 8 + z_lo), core: 2. Of those that a mesh axis runs over, the one named last changes fastest.
Arguments:
- inputs: bfloat16 [384, 5120], P('dp', 'tensor'), may hold values from -6 to 6
- w_gate: bfloat16 [5120, 27648], P('tensor', 'dp'), may hold values from -0.078125 to 0.078125
- w_up: bfloat16 [5120, 27648], P('tensor', 'dp'), may hold values from -0.078125 to 0.078125
- w_down: bfloat16 [27648, 5120], P('dp', 'tensor'), may hold values from -0.0390625 to 0.0390625
- out_grad: bfloat16 [384, 5120], P('dp', 'tensor'), may hold values from -6 to 6
- confidence: int32 [384], P('dp'), may hold values from 16 to 256
Outputs:
- grad_x: bfloat16 [384, 5120], P('dp', 'tensor')
- grad_gate: bfloat16 [5120, 27648], P('tensor', 'dp')
- grad_up: bfloat16 [5120, 27648], P('tensor', 'dp')
- grad_down: bfloat16 [27648, 5120], P('dp', 'tensor')
All inputs are finite; a program needn't handle non-finite values.
Results may differ from a plain program's by a relative error of at most 0.0057.
Values may be sent and summed in bfloat16 or wider, within the bound.
A program may use at most 64 MiB of HBM per device.

v0:
```python
import jax
import jax.numpy as jnp
from jax import lax
from jax.sharding import PartitionSpec as P


def over_rows(left, right):
    return lax.dot_general(
        left, right, (((0,), (0,)), ((), ())), preferred_element_type=jnp.float32
    )


def over_columns(left, right):
    return lax.dot_general(
        left, right, (((1,), (1,)), ((), ())), preferred_element_type=jnp.float32
    )


def swiglu_grads(totals, width):
    gate_pre = totals[:, :width]
    up_pre = totals[:, width : 2 * width]
    back_grad = totals[:, 2 * width :]
    logistic = jax.nn.sigmoid(gate_pre)
    swish = gate_pre * logistic
    hidden = (swish * up_pre).astype(jnp.bfloat16)
    up_grad = (back_grad * swish).astype(jnp.bfloat16)
    gate_grad = (back_grad * up_pre * logistic * (1.0 + gate_pre * (1.0 - logistic))).astype(
        jnp.bfloat16
    )
    return (hidden, gate_grad, up_grad)


def local(inputs, w_gate, w_up, w_down, out_grad, confidence):
    width = w_gate.shape[1]
    factor = confidence.astype(jnp.float32) / 256.0
    scaled = (out_grad.astype(jnp.float32) * factor[:, None]).astype(jnp.bfloat16)
    inputs_all, scaled_all = (
        lax.all_gather(inputs, "dp", axis=0, tiled=True),
        lax.all_gather(scaled, "dp", axis=0, tiled=True),
    )
    both_weights = jnp.concatenate([w_gate, w_up], axis=1)
    forward = jnp.dot(inputs_all, both_weights, preferred_element_type=jnp.float32)
    totals = lax.psum(
        jnp.concatenate([forward, over_columns(scaled_all, w_down)], axis=1), "tensor"
    )
    hidden, gate_grad, up_grad = swiglu_grads(totals, width)
    grad_down = over_rows(hidden, scaled_all).astype(jnp.bfloat16)
    grad_gate = over_rows(inputs_all, gate_grad).astype(jnp.bfloat16)
    grad_up = over_rows(inputs_all, up_grad).astype(jnp.bfloat16)
    grad_x = lax.psum_scatter(
        over_columns(gate_grad, w_gate) + over_columns(up_grad, w_up),
        "dp",
        scatter_dimension=0,
        tiled=True,
    ).astype(jnp.bfloat16)
    return (grad_x, grad_gate, grad_up, grad_down)


def solution(mesh):
    placed = (
        P("dp", "tensor"),
        P("tensor", "dp"),
        P("tensor", "dp"),
        P("dp", "tensor"),
        P("dp", "tensor"),
        P("dp"),
    )
    return jax.shard_map(
        local,
        mesh=mesh,
        in_specs=placed,
        out_specs=(P("dp", "tensor"), P("tensor", "dp"), P("tensor", "dp"), P("dp", "tensor")),
        check_vma=False,
    )
```

profile of v0, /device:TPU:6, one launch (start us, length us, event | category | flops | bytes accessed | tf_op | source)
XLA Modules:
  0.0 771.5 jit_solution(2201088023639936866)
XLA Ops:
  7.2 0.0 all-reduce.4.cloned.1.call-start
  7.2 154.3 %all-gather = bf16[32,12,320]{2,1,0:T(8,128)(2,1)S(1)} all-gather(bf16[1,12,320]{2,1,0:T(8,128)(2,1)} %bitcast.24), channel_id=1, replica_groups=mesh['dp'=32,'tensor'=16] {'dp'}, dimensions={0}, use_global_device_ids=true | all-gather | bytes 253440 | tf_op jit(solution)/shard_map/all_gather | solution.py:38
  161.6 0.1 reshape.10
  161.7 0.7 convert_multiply_fusion
  162.4 0.8 fusion.8
  163.1 148.5 %all-gather.1 = bf16[32,12,320]{2,1,0:T(8,128)(2,1)S(1)} all-gather(bf16[1,12,320]{2,1,0:T(8,128)(2,1)S(1)} %fusion.8), channel_id=1, replica_groups=mesh['dp'=32,'tensor'=16] {'dp'}, dimensions={0}, use_global_device_ids=true | all-gather | bytes 253440 | tf_op jit(solution)/shard_map/all_gather | solution.py:39
  311.6 0.1 reshape.12
  311.8 0.6 fusion.12
  312.4 0.3 copy-done.1
  312.7 0.3 copy-done.2
  313.0 1.5 convolution_bitcast_fusion
  314.5 2.1 pad_maximum_fusion
  316.6 0.0 all-reduce.4.cloned.1.call-update
  316.6 1.3 dynamic-slice.4
  318.5 223.6 %all-reduce.4.cloned.1.call-done = f32[384,2592]{0,1:T(8,128)} async-done(((f32[384,2592]{0,1:T(8,128)}), f32[384,2592]{0,1:T(8,128)}) %all-reduce.4.cloned.1.call-update) | async-done | bytes 3981328 | tf_op jit(solution)/shard_map/psum | solution.py:43
  542.1 2.7 multiply_convert_fusion.1
  544.8 0.6 fusion.13
  545.5 0.6 convolution_add_fusion
  546.1 165.5 %fusion = f32[16,320]{1,0:T(8,128)S(1)} fusion(f32[384,320]{1,0:T(8,128)S(1)} %convolution_add_fusion), kind=kCustom, calls=%all-reduce-scatter | all-reduce-scatter fusion | flops 163841 | bytes 514048
  711.6 2.8 collective-permute-start
  714.5 5.8 collective-permute-start.1
  720.2 9.9 %collective-permute-start.2 = (bf16[16,320]{1,0:T(8,128)(2,1)S(1)}, bf16[16,320]{1,0:T(8,128)(2,1)S(1)}, u32[]{:S(2)}, u32[]{:S(2)}) collective-permute-start(bf16[16,320]{1,0:T(8,128)(2,1)S(1)} %convert.14), channel_id=1, source_target_pairs={{0,48},{16,64},{32,80},{48,96},{64,112},{80,128},{96,144},{112,160... | collective-permute-start | bytes 30728
  730.1 6.4 collective-permute-start.3
  736.6 4.9 collective-permute-start.7
  741.5 3.2 convolution_convert_fusion
  744.7 1.4 fusion.2
  746.1 6.2 collective-permute-start.4
  752.3 4.3 collective-permute-start.5
  756.7 4.8 collective-permute-start.6
  761.5 1.4 fusion.3
  762.9 1.2 concatenate.8
  764.1 0.6 dynamic-slice_convert_fusion
  (16 shorter events, 0.1 us)
Async XLA Ops:
  7.2 304.6 %copy-start = (bf16[864,320]{0,1:T(8,128)(2,1)S(1)}, bf16[864,320]{0,1:T(8,128)(2,1)}, u32[]{:S(2)}) copy-start(bf16[864,320]{0,1:T(8,128)(2,1)} %param.9) | copy-start | bytes 1658884
  7.2 534.9 %all-reduce.4.cloned.1.call-start = ((), (), s32[]{:S(2)}) async-start(), calls=%async_computation | async-start | bytes 7962624 | tf_op jit(solution)/shard_map/psum | solution.py:43
  311.6 1.1 copy-start.1
  311.6 1.3 copy-start.2
  311.8 4.8 copy-start.3
  711.6 40.7 %collective-permute-start = (bf16[16,320]{1,0:T(8,128)(2,1)S(1)}, bf16[16,320]{1,0:T(8,128)(2,1)S(1)}, u32[]{:S(2)}, u32[]{:S(2)}) collective-permute-start(bf16[16,320]{1,0:T(8,128)(2,1)S(1)} %convert.14), channel_id=1, source_target_pairs={{0,16},{16,32},{32,48},{48,64},{64,80},{80,96},{96,112},{112,128},... | collective-permute-start | bytes 30728
  714.5 42.2 %collective-permute-start.1 = (bf16[16,320]{1,0:T(8,128)(2,1)S(1)}, bf16[16,320]{1,0:T(8,128)(2,1)S(1)}, u32[]{:S(2)}, u32[]{:S(2)}) collective-permute-start(bf16[16,320]{1,0:T(8,128)(2,1)S(1)} %convert.14), channel_id=1, source_target_pairs={{0,32},{16,48},{32,64},{48,80},{64,96},{80,112},{96,128},{112,144}... | collective-permute-start | bytes 30728
  720.2 42.6 %collective-permute-start.2 = (bf16[16,320]{1,0:T(8,128)(2,1)S(1)}, bf16[16,320]{1,0:T(8,128)(2,1)S(1)}, u32[]{:S(2)}, u32[]{:S(2)}) collective-permute-start(bf16[16,320]{1,0:T(8,128)(2,1)S(1)} %convert.14), channel_id=1, source_target_pairs={{0,48},{16,64},{32,80},{48,96},{64,112},{80,128},{96,144},{112,160... | collective-permute-start | bytes 30728
  730.1 32.7 %collective-permute-start.3 = (bf16[16,320]{1,0:T(8,128)(2,1)S(1)}, bf16[16,320]{1,0:T(8,128)(2,1)S(1)}, u32[]{:S(2)}, u32[]{:S(2)}) collective-permute-start(bf16[16,320]{1,0:T(8,128)(2,1)S(1)} %convert.14), channel_id=1, source_target_pairs={{0,64},{16,80},{32,96},{48,112},{64,128},{80,144},{96,160},{112,17... | collective-permute-start | bytes 30728
  736.6 9.5 %collective-permute-start.7 = (bf16[12,320]{1,0:T(8,128)(2,1)S(1)}, bf16[12,320]{1,0:T(8,128)(2,1)S(1)}, u32[]{:S(2)}, u32[]{:S(2)}) collective-permute-start(bf16[12,320]{1,0:T(8,128)(2,1)S(1)} %slice.15), channel_id=1, source_target_pairs={{0,128},{16,144},{32,160},{48,176},{64,192},{80,208},{96,224},{112... | collective-permute-start | bytes 23048
  746.1 16.7 %collective-permute-start.4 = (bf16[16,320]{1,0:T(8,128)(2,1)S(1)}, bf16[16,320]{1,0:T(8,128)(2,1)S(1)}, u32[]{:S(2)}, u32[]{:S(2)}) collective-permute-start(bf16[16,320]{1,0:T(8,128)(2,1)S(1)} %convert.14), channel_id=1, source_target_pairs={{0,80},{16,96},{32,112},{48,128},{64,144},{80,160},{96,176},{112,1... | collective-permute-start | bytes 30728
  752.3 10.5 %collective-permute-start.5 = (bf16[16,320]{1,0:T(8,128)(2,1)S(1)}, bf16[16,320]{1,0:T(8,128)(2,1)S(1)}, u32[]{:S(2)}, u32[]{:S(2)}) collective-permute-start(bf16[16,320]{1,0:T(8,128)(2,1)S(1)} %convert.14), channel_id=1, source_target_pairs={{0,96},{16,112},{32,128},{48,144},{64,160},{80,176},{96,192},{112,... | collective-permute-start | bytes 30728
  756.7 6.2 collective-permute-start.6
Sparse Core Ops, SparseCore 0:
  316.7 225.3 all-reduce.3
where the time goes:
time: 782 us; the launch traced here: 772 us
  blocking collectives  468 us (60%)
  waiting for transfers between devices  224 us (29%)
  starting transfers between devices  45.1 us (6%)
  between operations  14.9 us (2%)
  matrix products  9.33 us (1%)
    psum x1, waiting for transfers between devices, local(): lax.psum(jnp.concatenate([forward, over_columns(scaled_all, w_down)], axi...  224 us
    unnamed x1, blocking collectives  166 us
    all_gather x1, blocking collectives, local(): lax.all_gather(inputs, 'dp', axis=0, tiled=True)  154 us
    all_gather x1, blocking collectives, local(): lax.all_gather(scaled, 'dp', axis=0, tiled=True)  148 us
    unnamed x8, starting transfers between devices  45.1 us
  transfers between devices with their start and end apart: 9, of which 1 were waited for; matrix products, arithmetic and copies ran while one was open for 1% of the time, Pallas kernels for 0%

commit v1 on v0

v1 whole, which is shorter than its diff:
```python
import functools

import jax
import jax.numpy as jnp
import numpy as np
from jax import lax
from jax.experimental import pallas as pl
from jax.experimental.pallas import tpu as pltpu
from jax.sharding import PartitionSpec as P

BF16, F32 = jnp.bfloat16, jnp.float32
NY, NX, NH = 4, 4, 2
LINE = 8
LEFT, RIGHT = 3, 4
ROWS = 12
SLOT = 16
TOKENS = NY * NX * NH * ROWS
BLOCK = 16
BLOCKS = TOKENS // BLOCK
CHUNK = 128
MESH = pl.DeviceIdType.MESH


def contract(left, right, left_dim, right_dim):
    return lax.dot_general(
        left, right, (((left_dim,), (right_dim,)), ((), ())), preferred_element_type=F32
    )


def kernel(
    x_ref, s_ref, wg_ref, wu_ref, wd_ref, pick_ref, drop_ref,
    dx_ref, dg_ref, du_ref, dd_ref,
    xg, sg, xc, sc, wg_far, wu_far, wd_far, part, rin, rout, crs, res,
    gxc, gxp, rx, sy, ry, sz, rz,
    w_sem, g1_sem, g2_sem, g3_sem, c_sem,
    rs_send, rs_recv, cross_recv, ag_send, ag_recv, x1_sem, x2_sem, x3_sem,
):
    dp, tensor = lax.axis_index("dp"), lax.axis_index("tensor")
    y, x, h = dp // (NX * NH), (dp // NH) % NX, dp % NH
    z, core = tensor // 2, tensor % 2

    def at_dp(y_, x_, h_):
        return {"dp": (y_ * NX + x_) * NH + h_, "tensor": tensor}

    def at_line(z_, core_):
        return {"dp": dp, "tensor": z_ * 2 + core_}

    def remote(src, dst, send, recv, device):
        return pltpu.make_async_remote_copy(
            src_ref=src, dst_ref=dst, send_sem=send, recv_sem=recv,
            device_id=device, device_id_type=MESH,
        )

    across = at_dp(y, x, 1 - h)
    x_peers = [at_dp(y, (x + k) % NX, h) for k in range(1, NX)]
    y_peers = [at_dp((y + k) % NY, x, h) for k in range(1, NY)]
    sibling = at_line(z, 1 - core)

    xg[y, x, h] = x_ref[...]
    sg[y, x, h] = s_ref[...]

    barrier = pltpu.get_barrier_semaphore()

    def greet(device):
        pl.semaphore_signal(barrier, inc=1, device_id=device, device_id_type=MESH)

    for device in [across, sibling] + x_peers + y_peers:
        greet(device)

    @pl.when(z > 0)
    def _():
        greet(at_line(z - 1, 0))
        greet(at_line(z - 1, 1))

    @pl.when(z < LINE - 1)
    def _():
        greet(at_line(z + 1, 0))
        greet(at_line(z + 1, 1))

    fixed = 2 + (NX - 1) + (NY - 1)

    @pl.when((z == 0) | (z == LINE - 1))
    def _():
        pl.semaphore_wait(barrier, fixed + 2)

    @pl.when((z > 0) & (z < LINE - 1))
    def _():
        pl.semaphore_wait(barrier, fixed + 4)

    weights = [
        remote(src, dst, w_sem.at[0, i], w_sem.at[1, i], sibling)
        for i, (src, dst) in enumerate(
            [(wg_ref, wg_far), (wu_ref, wu_far), (wd_ref, wd_far)]
        )
    ]

    first = [
        remote(ref.at[y, x, h], ref.at[y, x, h], g1_sem.at[0, i], g1_sem.at[1, i], across)
        for i, ref in enumerate((xg, sg))
    ]
    for copy in first:
        copy.start()

    @pl.when(core == 1)
    def _():
        for copy in weights:
            copy.start()

    for copy in first:
        copy.wait_recv()
    second = []
    for k in range(1, NX):
        second.append(
            remote(xg.at[y, x], xg.at[y, x], g2_sem.at[0, 0, k - 1], g2_sem.at[1, 0, k - 1], x_peers[k - 1])
        )
        second.append(
            remote(sg.at[y, x], sg.at[y, x], g2_sem.at[0, 1, k - 1], g2_sem.at[1, 1, k - 1], y_peers[k - 1])
        )
    for copy in second:
        copy.start()
    for copy in second:
        copy.wait_recv()
    third = []
    for k in range(1, NX):
        third.append(
            remote(xg.at[y], xg.at[y], g3_sem.at[0, 0, k - 1], g3_sem.at[1, 0, k - 1], y_peers[k - 1])
        )
        third.append(
            remote(sg.at[:, x], sg.at[:, x], g3_sem.at[0, 1, k - 1], g3_sem.at[1, 1, k - 1], x_peers[k - 1])
        )
    for copy in third:
        copy.start()
    for copy in third:
        copy.wait_recv()

    half, half_slots = TOKENS // 2, NY * NX * NH * SLOT // 2
    for gathered, packed in ((xg, xc), (sg, sc)):
        for i in range(2):
            slots = gathered[pl.ds(i * NY // 2, NY // 2)].reshape(half_slots, -1)
            packed[0, pl.ds(i * half, half)] = contract(pick_ref[...], slots, 1, 0).astype(BF16)

    columns = [
        remote(packed.at[0], packed.at[1], c_sem.at[0, i], c_sem.at[1, i], sibling)
        for i, packed in enumerate((xc, sc))
    ]

    outer = jnp.where(z <= LEFT, z - 1, z + 1)
    inner = jnp.where(z <= LEFT, z + 1, z - 1)
    is_end = (z == 0) | (z == LINE - 1)
    is_mid = (z == LEFT) | (z == RIGHT)

    def rows_of(m):
        return pl.ds(pl.multiple_of(m * BLOCK, BLOCK), BLOCK)

    def mine(m):
        return (m % 2) == (z - LEFT)

    def onward(m):
        return remote(
            rout.at[:, rows_of(m)], rin.at[:, rows_of(m)], rs_send.at[m], rs_recv.at[m],
            at_line(inner, 0),
        )

    def cross(m):
        return remote(
            rout.at[:, rows_of(m)], crs.at[:, rows_of(m)], rs_send.at[m], cross_recv.at[m],
            at_line(inner, 0),
        )

    def result(m, i, device):
        here = res.at[:, rows_of(m)]
        return remote(here, here, ag_send.at[i, m], ag_recv.at[m], device)

    def each_block(body):
        def step(m, carry):
            body(m)
            return carry

        lax.fori_loop(0, BLOCKS, step, 0)

    @pl.when(core == 1)
    def _():
        for copy in columns:
            copy.start()

        def forward(m):
            result(m, 0, sibling).wait_recv()

            @pl.when(jnp.logical_not(is_mid & mine(m)))
            def _():
                @pl.when(jnp.logical_not(is_end))
                def _():
                    result(m, 1, at_line(outer, 1)).start()

                result(m, 0, sibling).start()

        each_block(forward)

        def drain(m):
            @pl.when(jnp.logical_not(is_mid & mine(m)))
            def _():
                @pl.when(jnp.logical_not(is_end))
                def _():
                    result(m, 1, at_line(outer, 1)).wait_send()

                result(m, 0, sibling).wait_send()

        each_block(drain)
        for copy in columns:
            copy.wait_send()
        for copy in weights:
            copy.wait_send()

    @pl.when(core == 0)
    def _():
        for copy in weights:
            copy.wait_recv()
        for copy in columns:
            copy.wait_recv()

        def products(i, carry):
            rows = pl.ds(pl.multiple_of(i * CHUNK, CHUNK), CHUNK)
            part[0, rows] = contract(xc[0, rows], wg_ref[...], 1, 0) + contract(
                xc[1, rows], wg_far[...], 1, 0
            )
            part[1, rows] = contract(xc[0, rows], wu_ref[...], 1, 0) + contract(
                xc[1, rows], wu_far[...], 1, 0
            )
            part[2, rows] = contract(sc[0, rows], wd_ref[...], 1, 1) + contract(
                sc[1, rows], wd_far[...], 1, 1
            )

            @pl.when(is_end)
            def _():
                def send(k, inside):
                    m = i * (CHUNK // BLOCK) + k
                    rout[:, rows_of(m)] = part[:, rows_of(m)].astype(BF16)
                    onward(m).start()
                    return inside

                lax.fori_loop(0, CHUNK // BLOCK, send, 0)

            return carry

        lax.fori_loop(0, TOKENS // CHUNK, products, 0)

        @pl.when(jnp.logical_not(is_end | is_mid))
        def _():
            def add(m):
                onward(m).wait_recv()
                rout[:, rows_of(m)] = (
                    part[:, rows_of(m)] + rin[:, rows_of(m)].astype(F32)
                ).astype(BF16)
                onward(m).start()

            each_block(add)

        @pl.when(is_mid)
        def _():
            def finish(m):
                cross(m).wait_recv()
                rows = rows_of(m)
                gate_pre, up_pre, back_grad = (
                    part[i, rows] + crs[i, rows].astype(F32) for i in range(3)
                )
                logistic = jax.nn.sigmoid(gate_pre)
                swish = gate_pre * logistic
                res[0, rows] = (swish * up_pre).astype(BF16)
                res[1, rows] = (
                    back_grad * up_pre * logistic * (1.0 + gate_pre * (1.0 - logistic))
                ).astype(BF16)
                res[2, rows] = (back_grad * swish).astype(BF16)
                result(m, 0, at_line(outer, 1)).start()
                result(m, 1, at_line(inner, 1)).start()
                result(m, 2, sibling).start()

            lag = 2

            def step(m, carry):
                @pl.when(m < BLOCKS)
                def _():
                    onward(m).wait_recv()
                    total = part[:, rows_of(m)] + rin[:, rows_of(m)].astype(F32)

                    @pl.when(mine(m))
                    def _():
                        part[:, rows_of(m)] = total

                    @pl.when(jnp.logical_not(mine(m)))
                    def _():
                        rout[:, rows_of(m)] = total.astype(BF16)
                        cross(m).start()

                @pl.when((m >= lag) & mine(m))
                def _():
                    finish(m - lag)

                return carry

            lax.fori_loop(0, BLOCKS + lag, step, 0)

        def take(m):
            @pl.when(jnp.logical_not(is_mid & mine(m)))
            def _():
                result(m, 0, sibling).wait_recv()

        each_block(take)

        def drain(m):
            @pl.when(is_mid & mine(m))
            def _():
                result(m, 0, at_line(outer, 1)).wait_send()
                result(m, 1, at_line(inner, 1)).wait_send()
                result(m, 2, sibling).wait_send()

            @pl.when(jnp.logical_not(is_mid & mine(m)))
            def _():
                onward(m).wait_send()

        each_block(drain)

    def back(i, carry):
        rows = pl.ds(pl.multiple_of(i * CHUNK, CHUNK), CHUNK)
        gxc[rows] = (
            contract(res[1, rows], wg_ref[...], 1, 1) + contract(res[2, rows], wu_ref[...], 1, 1)
        ).astype(BF16)
        return carry

    lax.fori_loop(0, TOKENS // CHUNK, back, 0)
    for i in range(2):
        gxp[pl.ds(i * NY // 2, NY // 2)] = (
            contract(drop_ref[...], gxc[pl.ds(i * half, half)], 1, 0)
            .astype(BF16)
            .reshape(NY // 2, NX, NH, SLOT, -1)
        )
    along_x = [
        remote(gxp.at[:, (x + k) % NX], rx.at[k - 1], x1_sem.at[0, k - 1], x1_sem.at[1, k - 1], x_peers[k - 1])
        for k in range(1, NX)
    ]
    for copy in along_x:
        copy.start()
    dg_ref[...] = contract(xc[0], res[1], 0, 0).astype(BF16)
    for copy in along_x:
        copy.wait_recv()
    sy[...] = gxp[:, x].astype(F32) + rx[0].astype(F32) + rx[1].astype(F32) + rx[2].astype(F32)
    along_y = [
        remote(sy.at[(y + k) % NY], ry.at[k - 1], x2_sem.at[0, k - 1], x2_sem.at[1, k - 1], y_peers[k - 1])
        for k in range(1, NY)
    ]
    for copy in along_y:
        copy.start()
    du_ref[...] = contract(xc[0], res[2], 0, 0).astype(BF16)
    for copy in along_y:
        copy.wait_recv()
    sz[...] = sy[y] + ry[0] + ry[1] + ry[2]
    last = remote(sz.at[1 - h], rz, x3_sem.at[0], x3_sem.at[1], across)
    last.start()
    dd_ref[...] = contract(res[0], sc[0], 0, 0).astype(BF16)
    last.wait_recv()
    dx_ref[...] = (sz[h] + rz[...])[:ROWS].astype(BF16)

    for copy in first + second + third + along_x + along_y + [last]:
        copy.wait_send()


def local(inputs, w_gate, w_up, w_down, out_grad, confidence):
    depth, width = w_gate.shape
    factor = confidence.astype(F32) / 256.0
    scaled = (out_grad.astype(F32) * factor[:, None]).astype(BF16)
    padding = ((0, SLOT - ROWS), (0, 0))
    half = TOKENS // 2
    row = np.arange(half)
    pick = np.zeros((half, half // ROWS * SLOT), np.float32)
    pick[row, row // ROWS * SLOT + row % ROWS] = 1.0
    vmem = pl.BlockSpec(memory_space=pltpu.VMEM)
    slots = (NY, NX, NH, SLOT, depth)
    wide = (3, TOKENS, width)
    return pl.pallas_call(
        kernel,
        out_shape=(
            jax.ShapeDtypeStruct(inputs.shape, BF16),
            jax.ShapeDtypeStruct(w_gate.shape, BF16),
            jax.ShapeDtypeStruct(w_up.shape, BF16),
            jax.ShapeDtypeStruct(w_down.shape, BF16),
        ),
        in_specs=[vmem] * 7,
        out_specs=(vmem,) * 4,
        scratch_shapes=[
            pltpu.VMEM(slots, BF16),
            pltpu.VMEM(slots, BF16),
            pltpu.VMEM((2, TOKENS, depth), BF16),
            pltpu.VMEM((2, TOKENS, depth), BF16),
            pltpu.VMEM((depth, width), BF16),
            pltpu.VMEM((depth, width), BF16),
            pltpu.VMEM((width, depth), BF16),
            pltpu.VMEM(wide, F32),
            pltpu.VMEM(wide, BF16),
            pltpu.VMEM(wide, BF16),
            pltpu.VMEM(wide, BF16),
            pltpu.VMEM(wide, BF16),
            pltpu.VMEM((TOKENS, depth), BF16),
            pltpu.VMEM(slots, BF16),
            pltpu.VMEM((NX - 1, NY, NH, SLOT, depth), BF16),
            pltpu.VMEM((NY, NH, SLOT, depth), F32),
            pltpu.VMEM((NY - 1, NH, SLOT, depth), F32),
            pltpu.VMEM((NH, SLOT, depth), F32),
            pltpu.VMEM((SLOT, depth), F32),
            pltpu.SemaphoreType.DMA((2, 3)),
            pltpu.SemaphoreType.DMA((2, 2)),
            pltpu.SemaphoreType.DMA((2, 2, NX - 1)),
            pltpu.SemaphoreType.DMA((2, 2, NX - 1)),
            pltpu.SemaphoreType.DMA((2, 2)),
            pltpu.SemaphoreType.DMA((BLOCKS,)),
            pltpu.SemaphoreType.DMA((BLOCKS,)),
            pltpu.SemaphoreType.DMA((BLOCKS,)),
            pltpu.SemaphoreType.DMA((3, BLOCKS)),
            pltpu.SemaphoreType.DMA((BLOCKS,)),
            pltpu.SemaphoreType.DMA((2, NX - 1)),
            pltpu.SemaphoreType.DMA((2, NY - 1)),
            pltpu.SemaphoreType.DMA((2,)),
        ],
        compiler_params=pltpu.CompilerParams(
            collective_id=0, has_side_effects=True, vmem_limit_bytes=48 << 20
        ),
        cost_estimate=pl.CostEstimate(
            flops=2 * TOKENS * depth * width * 11,
            bytes_accessed=12 * depth * width,
            transcendentals=0,
        ),
    )(
        jnp.pad(inputs, padding),
        jnp.pad(scaled, padding),
        w_gate,
        w_up,
        w_down,
        jnp.asarray(pick, BF16),
        jnp.asarray(pick.T, BF16),
    )


def solution(mesh):
    placed = (
        P("dp", "tensor"),
        P("tensor", "dp"),
        P("tensor", "dp"),
        P("dp", "tensor"),
        P("dp", "tensor"),
        P("dp"),
    )
    return jax.shard_map(
        local,
        mesh=mesh,
        in_specs=placed,
        out_specs=(P("dp", "tensor"), P("tensor", "dp"), P("tensor", "dp"), P("dp", "tensor")),
        check_vma=False,
    )
```

time: 782 us -> 129 us (0.16); the launches traced: 772 us -> 129 us
  blocking collectives: 468 us -> 0 us
  waiting for transfers between devices: 224 us -> 0 us
  Pallas kernels: 0 us -> 120 us
  starting transfers between devices: 45.1 us -> 0 us
  between operations: 14.9 us -> 0.71 us
  matrix products: 9.33 us -> 0 us
    all_gather x2 -> x0, blocking collectives: 303 us -> none  [the longest x1 154 us: local(): lax.all_gather(inputs, 'dp', axis=0, tiled=True)]
    psum x1 -> x0, waiting for transfers between devices: 224 us -> none  [local(): lax.psum(jnp.concatenate([forward, over_columns(scaled_all, w_down)], axi...]
    unnamed x1 -> x0, blocking collectives: 166 us -> none
    pallas_call x0 -> x1, Pallas kernels: none -> 120 us  [local(): pl.pallas_call(kernel, out_shape=(jax.ShapeDtypeStruct(inputs.shape, BF16...]
    unnamed x8 -> x0, starting transfers between devices: 45.1 us -> none
    dot_general x7 -> x0, matrix products: 9.33 us -> none  [the longest x3 5.98 us: over_rows(): lax.dot_general(left, right, (((0,), (0,)), ((), ())), preferred_element_...]
  transfers between devices with their start and end apart: 9 -> 0, of which waited for: 1 -> 0; matrix products, arithmetic and copies ran while one was open for 1% -> 0% of each run, Pallas kernels for 0% -> 0%
where the time goes in v1:
time: 129 us
  Pallas kernels  120 us (93%)
  local copies, waits for them, and re-layouts  6.54 us (5%)
  other arithmetic  1.44 us (1%)
    pallas_call x1, Pallas kernels, local(): pl.pallas_call(kernel, out_shape=(jax.ShapeDtypeStruct(inputs.shape, BF16...  120 us
    unnamed x14, local copies, waits for them, and re-layouts  5.45 us

profile of v1, /device:TPU:6, one launch (start us, length us, event | category | flops | bytes accessed | tf_op | source)
XLA Modules:
  0.0 129.1 jit_solution(16041311484112613469)
XLA Ops:
  0.6 0.7 convert_multiply_fusion
  1.3 0.8 multiply_convert_fusion
  2.1 0.0 copy-start.4
  2.1 0.7 copy-done.4
  2.8 0.0 copy-start
  2.8 0.0 copy-start.2
  2.8 0.0 copy-start.3
  2.8 1.5 %copy.12.wd_ref = bf16[864,320]{1,0:T(8,128)(2,1)S(1)} copy(bf16[864,320]{0,1:T(8,128)(2,1)} %param.11) | data formatting | bytes 1105920 | tf_op args[3]
  4.3 0.0 copy-done
  4.3 0.0 copy-done.2
  4.3 0.0 copy-done.3
  4.3 0.0 copy-start.1
  4.3 1.1 copy-done.1
  5.4 120.4 %shard_map.111 = (bf16[12,320]{1,0:T(8,128)(2,1)S(1)}, bf16[320,864]{1,0:T(8,128)(2,1)S(1)}, bf16[320,864]{1,0:T(8,128)(2,1)S(1)}, bf16[864,320]{1,0:T(8,128)(2,1)S(1)}) custom-call(bf16[16,320]{1,0:T(8,128)(2,1)S(1)} %pad.7.x_ref, bf16[16,320]{1,0:T(8,128)(2,1)S(1)} %pad.8.s_ref, bf16[320,864]{1,0:T(8,128)(2,1)S(1)} %copy-done, ...), custom_call_target="tpu_custom_call" | custom-call | flops 2335703040 | bytes 3317760 | tf_op jit(solution)/shard_map/pallas_call | solution.py:378
  125.8 1.1 copy.13
  126.8 0.6 copy.17
  127.4 0.8 copy.18
  128.3 0.8 copy.19
  (2 shorter events, 0.0 us)
Async XLA Ops:
  2.1 0.7 copy-start.4
  2.8 1.5 %copy-start = (bf16[320,864]{1,0:T(8,128)(2,1)S(1)}, bf16[320,864]{1,0:T(8,128)(2,1)}, u32[]{:S(2)}) copy-start(bf16[320,864]{1,0:T(8,128)(2,1)} %wg_ref.1) | copy-start | bytes 1658884
  2.8 1.5 %copy-start.2 = (bf16[256,192]{1,0:T(8,128)(2,1)S(1)}, bf16[256,192]{1,0:T(8,128)(2,1)}, u32[]{:S(2)}) copy-start(bf16[256,192]{1,0:T(8,128)(2,1)} %constant.11.clone.drop_ref) | copy-start | bytes 294916
  2.8 1.5 %copy-start.3 = (bf16[192,256]{1,0:T(8,128)(2,1)S(1)}, bf16[192,256]{1,0:T(8,128)(2,1)}, u32[]{:S(2)}) copy-start(bf16[192,256]{1,0:T(8,128)(2,1)} %constant.10.clone.pick_ref) | copy-start | bytes 294916
  4.3 1.1 copy-start.1

commit v2 on v0

v2 whole, which is shorter than its diff:
```python
import jax
import jax.numpy as jnp
import numpy as np
from jax import lax
from jax.experimental import pallas as pl
from jax.experimental.pallas import tpu as pltpu
from jax.sharding import PartitionSpec as P

BF16, F32 = jnp.bfloat16, jnp.float32
NY, NX, NH = 4, 4, 2
LINE = 8
LEFT, RIGHT = 3, 4
ROWS = 12
SLOT = 16
TOKENS = NY * NX * NH * ROWS
HALF = TOKENS // 2
BLOCK = 16
PAIRS = HALF // BLOCK // 2
BLOCKS = TOKENS // BLOCK
LEAD = 3
AG_LEAD = 2
MESH = pl.DeviceIdType.MESH


def contract(left, right, left_dim, right_dim):
    return lax.dot_general(
        left, right, (((left_dim,), (right_dim,)), ((), ())), preferred_element_type=F32
    )


def loop(start, stop, body):
    def step(i, carry):
        body(i)
        return carry

    lax.fori_loop(start, stop, step, 0)


def kernel(
    x_ref, og_ref, conf_ref, wg_hbm, wu_hbm, wd_hbm, pick_ref, drop_ref,
    dx_ref, dg_ref, du_ref, dd_ref,
    xb, sb, xg, sg, xc, sc, w, part, rin, rout, crs, res,
    gxp, rx, sy, ry, sz, rz,
    l_sem, w_sem, own_sem, z_sem, g1_sem, g2_sem, g3_sem, c_sem,
    rs_send, rs_recv, cross_recv, ag_send, ag_recv, x1_sem, x2_sem, x3_sem,
):
    dp, tensor = lax.axis_index("dp"), lax.axis_index("tensor")
    y, x, h = dp // (NX * NH), (dp // NH) % NX, dp % NH
    z, core = tensor // 2, tensor % 2

    def at_dp(y_, x_, h_, core_):
        return {"dp": (y_ * NX + x_) * NH + h_, "tensor": z * 2 + core_}

    def at_line(z_, core_):
        return {"dp": dp, "tensor": z_ * 2 + core_}

    def remote(src, dst, send, recv, device):
        return pltpu.make_async_remote_copy(
            src_ref=src, dst_ref=dst, send_sem=send, recv_sem=recv,
            device_id=device, device_id_type=MESH,
        )

    across = at_dp(y, x, 1 - h, core)
    x_peers = [at_dp(y, (x + k) % NX, h, core) for k in range(1, NX)]
    y_peers = [at_dp((y + k) % NY, x, h, core) for k in range(1, NY)]
    x_others = [at_dp(y, (x + k) % NX, h, 1 - core) for k in range(1, NX)]
    y_others = [at_dp((y + k) % NY, x, h, 1 - core) for k in range(1, NY)]
    sibling = at_line(z, 1 - core)

    barrier = pltpu.get_barrier_semaphore()

    def greet(device):
        pl.semaphore_signal(barrier, inc=1, device_id=device, device_id_type=MESH)

    greeted = [across, sibling] + x_peers + y_peers + x_others + y_others
    for device in greeted:
        greet(device)

    @pl.when(z > 0)
    def _():
        greet(at_line(z - 1, 0))
        greet(at_line(z - 1, 1))

    @pl.when(z < LINE - 1)
    def _():
        greet(at_line(z + 1, 0))
        greet(at_line(z + 1, 1))

    loads = [
        pltpu.make_async_copy(ref, w.at[0, i], l_sem.at[i])
        for i, ref in enumerate((wg_hbm, wu_hbm, wd_hbm))
    ]
    for copy in loads:
        copy.start()

    factor = conf_ref[...].astype(F32) / 256.0
    xb[...] = jnp.zeros_like(xb)
    sb[...] = jnp.zeros_like(sb)
    xb[pl.ds(0, ROWS)] = x_ref[...]
    sb[pl.ds(0, ROWS)] = (og_ref[...].astype(F32) * factor).astype(BF16)

    @pl.when(core == 1)
    def _():
        xg[0, y, x, 1] = xb[...]
        sg[0, y, x, 1] = sb[...]

    @pl.when((z == 0) | (z == LINE - 1))
    def _():
        pl.semaphore_wait(barrier, len(greeted) + 2)

    @pl.when((z > 0) & (z < LINE - 1))
    def _():
        pl.semaphore_wait(barrier, len(greeted) + 4)

    outer = jnp.where(z <= LEFT, z - 1, z + 1)
    inner = jnp.where(z <= LEFT, z + 1, z - 1)
    is_end = (z == 0) | (z == LINE - 1)
    is_mid = (z == LEFT) | (z == RIGHT)
    left_side = jnp.where(z <= LEFT, 1, 0)

    own = [
        remote(src, dst.at[0, y, x, 0], own_sem.at[0, i], own_sem.at[1, i], sibling)
        for i, (src, dst) in enumerate(((xb, xg), (sb, sg)))
    ]
    weights = remote(w.at[0], w.at[1], w_sem.at[0], w_sem.at[1], sibling)
    exchange = [
        remote(ref.at[0, y, x], ref.at[1, y, x], z_sem.at[0, i], z_sem.at[1, i], across)
        for i, ref in enumerate((xg, sg))
    ]

    def gather_first(half):
        copies = []
        for k in range(NX - 1):
            here = xg.at[half, y, x]
            copies.append(
                remote(here, here, g1_sem.at[half, 0, 0, k], g1_sem.at[half, 1, 0, k], x_peers[k])
            )
            here = sg.at[half, y, x]
            copies.append(
                remote(here, here, g1_sem.at[half, 0, 1, k], g1_sem.at[half, 1, 1, k], y_peers[k])
            )
        return copies

    def gather_last(half):
        copies = []
        for k in range(NX):
            here = xg.at[half, y]
            copies.append(
                remote(
                    here, here, g2_sem.at[half, 0, k], g2_sem.at[half, 1, k],
                    ([sibling] + y_others)[k],
                )
            )
            here = sg.at[half, :, x]
            copies.append(
                remote(
                    here, here, g3_sem.at[half, 0, k], g3_sem.at[half, 1, k],
                    ([sibling] + x_others)[k],
                )
            )
        return copies

    def half_rows(half):
        return pl.ds(half * HALF, HALF)

    def columns(half):
        return [
            remote(
                packed.at[1, half_rows(half)], packed.at[0, half_rows(half)],
                c_sem.at[half, 0, i], c_sem.at[half, 1, i], sibling,
            )
            for i, packed in enumerate((xc, sc))
        ]

    def rows_of(m):
        return pl.ds(pl.multiple_of(m * BLOCK, BLOCK), BLOCK)

    def mine(m):
        return (m % 2) == (z - LEFT)

    def onward(m):
        return remote(
            rout.at[:, rows_of(m)], rin.at[:, rows_of(m)], rs_send.at[m], rs_recv.at[m],
            at_line(inner, 0),
        )

    def cross(m):
        return remote(
            rout.at[:, rows_of(m)], crs.at[:, rows_of(m)], rs_send.at[m], cross_recv.at[m],
            at_line(inner, 0),
        )

    def result(m, i, device):
        here = res.at[:, rows_of(m)]
        return remote(here, here, ag_send.at[i, m], ag_recv.at[m], device)

    def along_x(half):
        return [
            remote(
                gxp.at[half, :, (x + k) % NX], rx.at[half, k - 1],
                x1_sem.at[half, 0, k - 1], x1_sem.at[half, 1, k - 1], x_peers[k - 1],
            )
            for k in range(1, NX)
        ]

    def along_y(half):
        return [
            remote(
                sy.at[half, (y + k) % NY], ry.at[half, k - 1],
                x2_sem.at[half, 0, k - 1], x2_sem.at[half, 1, k - 1], y_peers[k - 1],
            )
            for k in range(1, NY)
        ]

    def back(half):
        rows = half_rows(half)
        total = (
            contract(res[1, rows], w[0, 0], 1, 1) + contract(res[2, rows], w[0, 1], 1, 1)
        ).astype(BF16)
        gxp[half] = contract(drop_ref[...], total, 1, 0).astype(BF16).reshape(NY, NX, SLOT, -1)
        for copy in along_x(half):
            copy.start()

    def sum_x(half):
        for copy in along_x(half):
            copy.wait_recv()
        total = gxp[half, :, x].astype(F32)
        for k in range(NX - 1):
            total = total + rx[half, k].astype(F32)
        sy[half] = total
        for copy in along_y(half):
            copy.start()

    def sum_y(half):
        for copy in along_y(half):
            copy.wait_recv()
        total = sy[half, y]
        for k in range(NY - 1):
            total = total + ry[half, k]
        sz[half] = total

    @pl.when(core == 1)
    def _():
        for copy in own:
            copy.wait_recv()
        for copy in gather_first(0) + exchange:
            copy.start()
        for copy in loads:
            copy.wait()
        weights.start()
        for copy in gather_first(0):
            copy.wait_recv()
        for copy in gather_last(0):
            copy.start()
        for copy in exchange:
            copy.wait_recv()
        for copy in gather_first(1):
            copy.start()
        for copy in gather_first(1):
            copy.wait_recv()
        for copy in gather_last(1):
            copy.start()

        def forward(m):
            result(m, 0, sibling).wait_recv()

            @pl.when(jnp.logical_not(is_mid & mine(m)))
            def _():
                @pl.when(jnp.logical_not(is_end))
                def _():
                    result(m, 1, at_line(outer, 1)).start()

                result(m, 0, sibling).start()

        for half in range(2):

            def step(s):
                @pl.when(s < PAIRS)
                def _():
                    forward(2 * (half * PAIRS + s) + 1 - left_side)

                @pl.when(s >= AG_LEAD)
                def _():
                    forward(2 * (half * PAIRS + s - AG_LEAD) + left_side)

            loop(0, PAIRS + AG_LEAD, step)
            back(half)

        for half in range(2):
            for copy in columns(half):
                copy.wait_recv()

    @pl.when(core == 0)
    def _():
        for copy in own:
            copy.start()

        def finish(m):
            onward(m).wait_recv()
            cross(m).wait_recv()
            rows = rows_of(m)
            gate_pre, up_pre, back_grad = (
                part[i, rows] + rin[i, rows].astype(F32) + crs[i, rows].astype(F32)
                for i in range(3)
            )
            logistic = jax.nn.sigmoid(gate_pre)
            swish = gate_pre * logistic
            res[0, rows] = (swish * up_pre).astype(BF16)
            res[1, rows] = (
                back_grad * up_pre * logistic * (1.0 + gate_pre * (1.0 - logistic))
            ).astype(BF16)
            res[2, rows] = (back_grad * swish).astype(BF16)
            result(m, 0, at_line(outer, 1)).start()
            result(m, 1, at_line(inner, 1)).start()
            result(m, 2, sibling).start()

        def add(m):
            @pl.when(is_end)
            def _():
                rout[:, rows_of(m)] = part[:, rows_of(m)].astype(BF16)
                onward(m).start()

            @pl.when(jnp.logical_not(is_end))
            def _():
                onward(m).wait_recv()
                rout[:, rows_of(m)] = (
                    part[:, rows_of(m)] + rin[:, rows_of(m)].astype(F32)
                ).astype(BF16)

                @pl.when(is_mid)
                def _():
                    cross(m).start()

                @pl.when(jnp.logical_not(is_mid))
                def _():
                    onward(m).start()

        for half in range(2):
            for copy in gather_last(half):
                copy.wait_recv()
            rows = half_rows(half)
            for gathered, packed in ((xg, xc), (sg, sc)):
                for side in range(2):
                    slots = gathered[half, :, :, side].reshape(NY * NX * SLOT, -1)
                    packed[side, rows] = contract(pick_ref[...], slots, 1, 0).astype(BF16)
            for copy in columns(half):
                copy.start()
            if half == 0:
                for copy in loads:
                    copy.wait()
                weights.wait_recv()
            for i, packed in enumerate((xc, xc, sc)):
                part[i, rows] = contract(packed[0, rows], w[0, i], 1, 0) + contract(
                    packed[1, rows], w[1, i], 1, 0
                )

            def step(s):
                @pl.when(s < PAIRS)
                def _():
                    add(2 * (half * PAIRS + s) + left_side)

                @pl.when(s >= LEAD)
                def _():
                    m = 2 * (half * PAIRS + s - LEAD) + 1 - left_side

                    @pl.when(is_mid)
                    def _():
                        finish(m)

                    @pl.when(jnp.logical_not(is_mid))
                    def _():
                        add(m)

            loop(0, PAIRS + LEAD, step)

        for half in range(2):

            def take(i):
                m = half * 2 * PAIRS + i

                @pl.when(jnp.logical_not(is_mid & mine(m)))
                def _():
                    result(m, 0, sibling).wait_recv()

            loop(0, 2 * PAIRS, take)
            back(half)

    sum_x(0)
    dg_ref[...] = contract(xc[0], res[1], 0, 0).astype(BF16)
    sum_x(1)
    du_ref[...] = contract(xc[0], res[2], 0, 0).astype(BF16)
    sum_y(1)
    last = remote(sz.at[1], rz, x3_sem.at[0], x3_sem.at[1], across)
    last.start()
    sum_y(0)
    dd_ref[...] = contract(sc[0], res[0], 0, 0).astype(BF16)

    @pl.when(core == 1)
    def _():
        for copy in exchange + [weights]:
            copy.wait_send()
        for half in range(2):
            for copy in gather_first(half) + gather_last(half):
                copy.wait_send()

        def drain(m):
            @pl.when(jnp.logical_not(is_mid & mine(m)))
            def _():
                @pl.when(jnp.logical_not(is_end))
                def _():
                    result(m, 1, at_line(outer, 1)).wait_send()

                result(m, 0, sibling).wait_send()

        loop(0, BLOCKS, drain)

    @pl.when(core == 0)
    def _():
        for copy in own:
            copy.wait_send()
        for half in range(2):
            for copy in columns(half):
                copy.wait_send()

        def drain(m):
            @pl.when(is_mid & mine(m))
            def _():
                result(m, 0, at_line(outer, 1)).wait_send()
                result(m, 1, at_line(inner, 1)).wait_send()
                result(m, 2, sibling).wait_send()

            @pl.when(jnp.logical_not(is_mid & mine(m)))
            def _():
                onward(m).wait_send()

        loop(0, BLOCKS, drain)

    for half in range(2):
        for copy in along_x(half) + along_y(half):
            copy.wait_send()
    last.wait()
    dx_ref[...] = (sz[0] + rz[...])[:ROWS].astype(BF16)


def local(inputs, w_gate, w_up, w_down, out_grad, confidence):
    depth, width = w_gate.shape
    row = np.arange(HALF)
    pick = np.zeros((HALF, HALF // ROWS * SLOT), np.float32)
    pick[row, row // ROWS * SLOT + row % ROWS] = 1.0
    vmem = pl.BlockSpec(memory_space=pltpu.VMEM)
    hbm = pl.BlockSpec(memory_space=pl.ANY)
    slots = (2, NY, NX, 2, SLOT, depth)
    wide = (3, TOKENS, width)
    dma = pltpu.SemaphoreType.DMA
    grad_x, grad_gate, grad_up, grad_down = pl.pallas_call(
        kernel,
        out_shape=(
            jax.ShapeDtypeStruct(inputs.shape, BF16),
            jax.ShapeDtypeStruct(w_gate.shape, BF16),
            jax.ShapeDtypeStruct(w_up.shape, BF16),
            jax.ShapeDtypeStruct((depth, width), BF16),
        ),
        in_specs=[vmem] * 3 + [hbm] * 3 + [vmem] * 2,
        out_specs=(vmem,) * 4,
        scratch_shapes=[
            pltpu.VMEM((SLOT, depth), BF16),
            pltpu.VMEM((SLOT, depth), BF16),
            pltpu.VMEM(slots, BF16),
            pltpu.VMEM(slots, BF16),
            pltpu.VMEM((2, TOKENS, depth), BF16),
            pltpu.VMEM((2, TOKENS, depth), BF16),
            pltpu.VMEM((2, 3, depth, width), BF16),
            pltpu.VMEM(wide, F32),
            pltpu.VMEM(wide, BF16),
            pltpu.VMEM(wide, BF16),
            pltpu.VMEM(wide, BF16),
            pltpu.VMEM(wide, BF16),
            pltpu.VMEM((2, NY, NX, SLOT, depth), BF16),
            pltpu.VMEM((2, NX - 1, NY, SLOT, depth), BF16),
            pltpu.VMEM((2, NY, SLOT, depth), F32),
            pltpu.VMEM((2, NY - 1, SLOT, depth), F32),
            pltpu.VMEM((2, SLOT, depth), F32),
            pltpu.VMEM((SLOT, depth), F32),
            dma((3,)),
            dma((2,)),
            dma((2, 2)),
            dma((2, 2)),
            dma((2, 2, 2, NX - 1)),
            dma((2, 2, NX)),
            dma((2, 2, NX)),
            dma((2, 2, 2)),
            dma((BLOCKS,)),
            dma((BLOCKS,)),
            dma((BLOCKS,)),
            dma((3, BLOCKS)),
            dma((BLOCKS,)),
            dma((2, 2, NX - 1)),
            dma((2, 2, NY - 1)),
            dma((2,)),
        ],
        compiler_params=pltpu.CompilerParams(
            collective_id=0, has_side_effects=True, vmem_limit_bytes=52 << 20
        ),
        cost_estimate=pl.CostEstimate(
            flops=2 * TOKENS * depth * width * 11,
            bytes_accessed=12 * depth * width,
            transcendentals=0,
        ),
    )(
        inputs,
        out_grad,
        confidence[:, None],
        w_gate,
        w_up,
        w_down.T,
        jnp.asarray(pick, BF16),
        jnp.asarray(pick.T, BF16),
    )
    return grad_x, grad_gate, grad_up, grad_down.T


def solution(mesh):
    placed = (
        P("dp", "tensor"),
        P("tensor", "dp"),
        P("tensor", "dp"),
        P("dp", "tensor"),
        P("dp", "tensor"),
        P("dp"),
    )
    return jax.shard_map(
        local,
        mesh=mesh,
        in_specs=placed,
        out_specs=(P("dp", "tensor"), P("tensor", "dp"), P("tensor", "dp"), P("dp", "tensor")),
        check_vma=False,
    )
```

time: 782 us -> 99.3 us (0.13); the launches traced: 772 us -> 98.5 us
  blocking collectives: 468 us -> 0 us
  waiting for transfers between devices: 224 us -> 0 us
  Pallas kernels: 0 us -> 91.6 us
  starting transfers between devices: 45.1 us -> 0 us
  between operations: 14.9 us -> 0.65 us
  matrix products: 9.33 us -> 0 us
    all_gather x2 -> x0, blocking collectives: 303 us -> none  [the longest x1 154 us: local(): lax.all_gather(inputs, 'dp', axis=0, tiled=True)]
    psum x1 -> x0, waiting for transfers between devices: 224 us -> none  [local(): lax.psum(jnp.concatenate([forward, over_columns(scaled_all, w_down)], axi...]
    unnamed x1 -> x0, blocking collectives: 166 us -> none
    pallas_call x0 -> x1, Pallas kernels: none -> 91.6 us  [local(): pl.pallas_call(kernel, out_shape=(jax.ShapeDtypeStruct(inputs.shape, BF16...]
    unnamed x8 -> x0, starting transfers between devices: 45.1 us -> none
    dot_general x7 -> x0, matrix products: 9.33 us -> none  [the longest x3 5.98 us: over_rows(): lax.dot_general(left, right, (((0,), (0,)), ((), ())), preferred_element_...]
  transfers between devices with their start and end apart: 9 -> 0, of which waited for: 1 -> 0; matrix products, arithmetic and copies ran while one was open for 1% -> 0% of each run, Pallas kernels for 0% -> 0%
where the time goes in v2:
time: 99.3 us; the launch traced here: 98.5 us
  Pallas kernels  91.6 us (92%)
  local copies, waits for them, and re-layouts  6.29 us (6%)
    pallas_call x1, Pallas kernels, local(): pl.pallas_call(kernel, out_shape=(jax.ShapeDtypeStruct(inputs.shape, BF16...  91.6 us
    unnamed x12, local copies, waits for them, and re-layouts  5.54 us

profile of v2, /device:TPU:6, one launch (start us, length us, event | category | flops | bytes accessed | tf_op | source)
XLA Modules:
  0.0 98.5 jit_solution(3054859296260249785)
XLA Ops:
  0.6 0.0 copy-start
  0.6 0.7 copy.12.conf_ref
  1.4 0.0 copy-done
  1.4 0.0 copy-start.1
  1.4 0.7 copy-done.1
  2.1 0.0 copy-start.2
  2.1 0.9 copy-done.2
  3.0 0.0 copy-start.3
  3.0 0.9 copy-done.3
  3.9 91.6 %shard_map.111 = (bf16[12,320]{1,0:T(8,128)(2,1)S(1)}, bf16[320,864]{1,0:T(8,128)(2,1)S(1)}, bf16[320,864]{1,0:T(8,128)(2,1)S(1)}, bf16[320,864]{1,0:T(8,128)(2,1)S(1)}) custom-call(bf16[12,320]{1,0:T(8,128)(2,1)S(1)} %copy-done, bf16[12,320]{1,0:T(8,128)(2,1)S(1)} %copy-done.1, s32[12,1]{1,0:T(8,128)S(1)} %copy.12.conf_ref, bf16[320,864]{1,0:T(8,128)(2,1)} %wg_hbm.1, ...), custom_call_target="tpu_custom_call" | custom-call | flops 2335703040 | bytes 3317760 | tf_op jit(solution)/shard_map/pallas_call | solution.py:455
  95.5 0.6 copy.17
  96.1 0.8 copy.18
  96.9 0.8 copy.19
  97.7 0.8 copy.20
Async XLA Ops:
  0.6 0.8 copy-start
  1.4 0.7 copy-start.1
  2.1 0.9 copy-start.2
  3.0 0.9 copy-start.3

commit v3 on v2

--- a/solution.py
+++ b/solution.py
@@ -15,10 +15,11 @@
 TOKENS = NY * NX * NH * ROWS
 HALF = TOKENS // 2
 BLOCK = 16
-PAIRS = HALF // BLOCK // 2
 BLOCKS = TOKENS // BLOCK
-LEAD = 3
-AG_LEAD = 2
+PAIRS = BLOCKS // 2
+CUTS = (0, PAIRS // 4, 3 * PAIRS // 4, PAIRS)
+LEAD = 2
+MATRICES = 3
 MESH = pl.DeviceIdType.MESH
 
 
@@ -160,45 +161,48 @@
             )
         return copies
 
-    def half_rows(half):
-        return pl.ds(half * HALF, HALF)
-
-    def columns(half):
+    columns = [
+        remote(packed.at[1], packed.at[0], c_sem.at[0, i], c_sem.at[1, i], sibling)
+        for i, packed in enumerate((xc, sc))
+    ]
+
+    def segment(i):
+        start, stop = CUTS[i] * 2 * BLOCK, CUTS[i + 1] * 2 * BLOCK
+        slots = (pl.ds(0, NY // 2), pl.ds(0, NY), pl.ds(NY // 2, NY // 2))[i]
+        return pl.ds(start, stop - start), i % 2, slots, stop - start
+
+    def rows_of(m):
+        return pl.ds(pl.multiple_of(m * BLOCK, BLOCK), BLOCK)
+
+    def mine(m):
+        return (m % 2) == (z - LEFT)
+
+    def onward(m, i):
+        return remote(
+            rout.at[i, rows_of(m)], rin.at[i, rows_of(m)], rs_send, rs_recv.at[m, i],
+            at_line(inner, 0),
+        )
+
+    def cross(m, i):
+        return remote(
+            rout.at[i, rows_of(m)], crs.at[i, rows_of(m)], rs_send, cross_recv.at[m, i],
+            at_line(inner, 0),
+        )
+
+    def result(m, i, way, device):
+        here = res.at[i, rows_of(m)]
+        return remote(here, here, ag_send.at[way], ag_recv.at[m, i], device)
+
+    def sent(buffer, blocks, sem):
+        rows = buffer.at[:, pl.ds(0, blocks * BLOCK)]
+        remote(rows, rows, sem, sem, sibling).wait_send()
+
+    def along_x(i):
+        _, half, slots, _ = segment(i)
         return [
             remote(
-                packed.at[1, half_rows(half)], packed.at[0, half_rows(half)],
-                c_sem.at[half, 0, i], c_sem.at[half, 1, i], sibling,
-            )
-            for i, packed in enumerate((xc, sc))
-        ]
-
-    def rows_of(m):
-        return pl.ds(pl.multiple_of(m * BLOCK, BLOCK), BLOCK)
-
-    def mine(m):
-        return (m % 2) == (z - LEFT)
-
-    def onward(m):
-        return remote(
-            rout.at[:, rows_of(m)], rin.at[:, rows_of(m)], rs_send.at[m], rs_recv.at[m],
-            at_line(inner, 0),
-        )
-
-    def cross(m):
-        return remote(
-            rout.at[:, rows_of(m)], crs.at[:, rows_of(m)], rs_send.at[m], cross_recv.at[m],
-            at_line(inner, 0),
-        )
-
-    def result(m, i, device):
-        here = res.at[:, rows_of(m)]
-        return remote(here, here, ag_send.at[i, m], ag_recv.at[m], device)
-
-    def along_x(half):
-        return [
-            remote(
-                gxp.at[half, :, (x + k) % NX], rx.at[half, k - 1],
-                x1_sem.at[half, 0, k - 1], x1_sem.at[half, 1, k - 1], x_peers[k - 1],
+                gxp.at[half, slots, (x + k) % NX], rx.at[half, k - 1, slots],
+                x1_sem.at[i, 0, k - 1], x1_sem.at[i, 1, k - 1], x_peers[k - 1],
             )
             for k in range(1, NX)
         ]
@@ -212,18 +216,24 @@
             for k in range(1, NY)
         ]
 
-    def back(half):
-        rows = half_rows(half)
+    def back(i):
+        rows, half, slots, size = segment(i)
         total = (
             contract(res[1, rows], w[0, 0], 1, 1) + contract(res[2, rows], w[0, 1], 1, 1)
         ).astype(BF16)
-        gxp[half] = contract(drop_ref[...], total, 1, 0).astype(BF16).reshape(NY, NX, SLOT, -1)
-        for copy in along_x(half):
+        padded = size // ROWS * SLOT
+        gxp[half, slots] = (
+            contract(drop_ref[pl.ds(0, padded), pl.ds(0, size)], total, 1, 0)
+            .astype(BF16)
+            .reshape(-1, NX, SLOT, total.shape[-1])
+        )
+        for copy in along_x(i):
             copy.start()
 
     def sum_x(half):
-        for copy in along_x(half):
-            copy.wait_recv()
+        for i in (0, 2) if half == 0 else (1,):
+            for copy in along_x(i):
+                copy.wait_recv()
         total = gxp[half, :, x].astype(F32)
         for k in range(NX - 1):
             total = total + rx[half, k].astype(F32)
@@ -262,106 +272,110 @@
             copy.start()
 
         def forward(m):
-            result(m, 0, sibling).wait_recv()
-
-            @pl.when(jnp.logical_not(is_mid & mine(m)))
+            for i in range(MATRICES):
+                result(m, i, 0, sibling).wait_recv()
+
+                @pl.when(jnp.logical_not(is_mid & mine(m)))
+                def _():
+                    result(m, i, 0, sibling).start()
+
+                    @pl.when(jnp.logical_not(is_end))
+                    def _():
+                        result(m, i, 1, at_line(outer, 1)).start()
+
+        def step(s):
+            @pl.when(s < PAIRS)
             def _():
+                forward(2 * s + 1 - left_side)
+
+            @pl.when(s >= LEAD)
+            def _():
+                forward(2 * (s - LEAD) + left_side)
+
+        loop(0, CUTS[1] + LEAD, step)
+        back(0)
+        loop(CUTS[1] + LEAD, CUTS[2] + LEAD, step)
+        back(1)
+        loop(CUTS[2] + LEAD, PAIRS, step)
+        sum_x(1)
+        loop(PAIRS, PAIRS + LEAD, step)
+        back(2)
+        for copy in columns:
+            copy.wait_recv()
+
+    @pl.when(core == 0)
+    def _():
+        for copy in own:
+            copy.start()
+
+        def finish(m):
+            rows = rows_of(m)
+            totals = []
+            for i in range(MATRICES):
+                onward(m, i).wait_recv()
+                cross(m, i).wait_recv()
+                totals.append(
+                    part[i, rows] + rin[i, rows].astype(F32) + crs[i, rows].astype(F32)
+                )
+            gate_pre, up_pre, back_grad = totals
+            logistic = jax.nn.sigmoid(gate_pre)
+            swish = gate_pre * logistic
+            gate_grad = back_grad * up_pre * logistic * (1.0 + gate_pre * (1.0 - logistic))
+            for i, value in enumerate((swish * up_pre, gate_grad, back_grad * swish)):
+                res[i, rows] = value.astype(BF16)
+                result(m, i, 0, at_line(outer, 1)).start()
+                result(m, i, 1, at_line(inner, 1)).start()
+                result(m, i, 2, sibling).start()
+
+        def add(m):
+            rows = rows_of(m)
+            for i in range(MATRICES):
+
+                @pl.when(is_end)
+                def _():
+                    rout[i, rows] = part[i, rows].astype(BF16)
+                    onward(m, i).start()
+
                 @pl.when(jnp.logical_not(is_end))
                 def _():
-                    result(m, 1, at_line(outer, 1)).start()
-
-                result(m, 0, sibling).start()
-
-        for half in range(2):
-
-            def step(s):
-                @pl.when(s < PAIRS)
-                def _():
-                    forward(2 * (half * PAIRS + s) + 1 - left_side)
-
-                @pl.when(s >= AG_LEAD)
-                def _():
-                    forward(2 * (half * PAIRS + s - AG_LEAD) + left_side)
-
-            loop(0, PAIRS + AG_LEAD, step)
-            back(half)
-
-        for half in range(2):
-            for copy in columns(half):
-                copy.wait_recv()
-
-    @pl.when(core == 0)
-    def _():
-        for copy in own:
-            copy.start()
-
-        def finish(m):
-            onward(m).wait_recv()
-            cross(m).wait_recv()
-            rows = rows_of(m)
-            gate_pre, up_pre, back_grad = (
-                part[i, rows] + rin[i, rows].astype(F32) + crs[i, rows].astype(F32)
-                for i in range(3)
-            )
-            logistic = jax.nn.sigmoid(gate_pre)
-            swish = gate_pre * logistic
-            res[0, rows] = (swish * up_pre).astype(BF16)
-            res[1, rows] = (
-                back_grad * up_pre * logistic * (1.0 + gate_pre * (1.0 - logistic))
-            ).astype(BF16)
-            res[2, rows] = (back_grad * swish).astype(BF16)
-            result(m, 0, at_line(outer, 1)).start()
-            result(m, 1, at_line(inner, 1)).start()
-            result(m, 2, sibling).start()
-
-        def add(m):
-            @pl.when(is_end)
-            def _():
-                rout[:, rows_of(m)] = part[:, rows_of(m)].astype(BF16)
-                onward(m).start()
-
-            @pl.when(jnp.logical_not(is_end))
-            def _():
-                onward(m).wait_recv()
-                rout[:, rows_of(m)] = (
-                    part[:, rows_of(m)] + rin[:, rows_of(m)].astype(F32)
-                ).astype(BF16)
-
-                @pl.when(is_mid)
-                def _():
-                    cross(m).start()
-
-                @pl.when(jnp.logical_not(is_mid))
-                def _():
-                    onward(m).start()
-
-        for half in range(2):
-            for copy in gather_last(half):
-                copy.wait_recv()
-            rows = half_rows(half)
+                    onward(m, i).wait_recv()
+                    rout[i, rows] = (part[i, rows] + rin[i, rows].astype(F32)).astype(BF16)
+
+                    @pl.when(is_mid)
+                    def _():
+                        cross(m, i).start()
+
+                    @pl.when(jnp.logical_not(is_mid))
+                    def _():
+                        onward(m, i).start()
+
+        def products(i):
+            rows, half, slots, size = segment(i)
+            padded = size // ROWS * SLOT
             for gathered, packed in ((xg, xc), (sg, sc)):
                 for side in range(2):
-                    slots = gathered[half, :, :, side].reshape(NY * NX * SLOT, -1)
-                    packed[side, rows] = contract(pick_ref[...], slots, 1, 0).astype(BF16)
-            for copy in columns(half):
-                copy.start()
-            if half == 0:
+                    block = gathered[half, slots, :, side].reshape(padded, -1)
+                    packed[side, rows] = contract(
+                        pick_ref[pl.ds(0, size), pl.ds(0, padded)], block, 1, 0
+                    ).astype(BF16)
+            if i == 0:
                 for copy in loads:
                     copy.wait()
                 weights.wait_recv()
-            for i, packed in enumerate((xc, xc, sc)):
-                part[i, rows] = contract(packed[0, rows], w[0, i], 1, 0) + contract(
-                    packed[1, rows], w[1, i], 1, 0
+            for j, packed in enumerate((xc, xc, sc)):
+                part[j, rows] = contract(packed[0, rows], w[0, j], 1, 0) + contract(
+                    packed[1, rows], w[1, j], 1, 0
                 )
 
+        def stream(first, last):
             def step(s):
-                @pl.when(s < PAIRS)
+                @pl.when(s < last)
                 def _():
-                    add(2 * (half * PAIRS + s) + left_side)
-
-                @pl.when(s >= LEAD)
+                    add(2 * s + left_side)
+
+                @pl.when(s >= first + LEAD)
                 def _():
-                    m = 2 * (half * PAIRS + s - LEAD) + 1 - left_side
+                    m = 2 * (s - LEAD) + 1 - left_side
 
                     @pl.when(is_mid)
                     def _():
@@ -371,27 +385,38 @@
                     def _():
                         add(m)
 
-            loop(0, PAIRS + LEAD, step)
-
-        for half in range(2):
-
-            def take(i):
-                m = half * 2 * PAIRS + i
-
-                @pl.when(jnp.logical_not(is_mid & mine(m)))
-                def _():
-                    result(m, 0, sibling).wait_recv()
-
-            loop(0, 2 * PAIRS, take)
-            back(half)
-
-    sum_x(0)
-    dg_ref[...] = contract(xc[0], res[1], 0, 0).astype(BF16)
-    sum_x(1)
-    du_ref[...] = contract(xc[0], res[2], 0, 0).astype(BF16)
+            loop(first, last + LEAD, step)
+
+        for copy in gather_last(0):
+            copy.wait_recv()
+        products(0)
+        stream(CUTS[0], CUTS[1])
+        products(2)
+        for copy in gather_last(1):
+            copy.wait_recv()
+        products(1)
+        stream(CUTS[1], CUTS[3])
+        for copy in columns:
+            copy.start()
+
+        def take(m):
+            @pl.when(jnp.logical_not(is_mid & mine(m)))
+            def _():
+                for i in range(MATRICES):
+                    result(m, i, 0, sibling).wait_recv()
+
+        for i in range(3):
+            loop(2 * CUTS[i], 2 * CUTS[i + 1], take)
+            back(i)
+            if i == 1:
+                sum_x(1)
+
     sum_y(1)
     last = remote(sz.at[1], rz, x3_sem.at[0], x3_sem.at[1], across)
     last.start()
+    dg_ref[...] = contract(xc[0], res[1], 0, 0).astype(BF16)
+    sum_x(0)
+    du_ref[...] = contract(xc[0], res[2], 0, 0).astype(BF16)
     sum_y(0)
     dd_ref[...] = contract(sc[0], res[0], 0, 0).astype(BF16)
 
@@ -403,40 +428,39 @@
             for copy in gather_first(half) + gather_last(half):
                 copy.wait_send()
 
-        def drain(m):
-            @pl.when(jnp.logical_not(is_mid & mine(m)))
+        @pl.when(is_mid)
+        def _():
+            sent(res, BLOCKS // 2, ag_send.at[0])
+            sent(res, BLOCKS // 2, ag_send.at[1])
+
+        @pl.when(jnp.logical_not(is_mid))
+        def _():
+            sent(res, BLOCKS, ag_send.at[0])
+
+            @pl.when(jnp.logical_not(is_end))
             def _():
-                @pl.when(jnp.logical_not(is_end))
-                def _():
-                    result(m, 1, at_line(outer, 1)).wait_send()
-
-                result(m, 0, sibling).wait_send()
-
-        loop(0, BLOCKS, drain)
+                sent(res, BLOCKS, ag_send.at[1])
 
     @pl.when(core == 0)
     def _():
-        for copy in own:
+        for copy in own + columns:
             copy.wait_send()
-        for half in range(2):
-            for copy in columns(half):
-                copy.wait_send()
-
-        def drain(m):
-            @pl.when(is_mid & mine(m))
-            def _():
-                result(m, 0, at_line(outer, 1)).wait_send()
-                result(m, 1, at_line(inner, 1)).wait_send()
-                result(m, 2, sibling).wait_send()
-
-            @pl.when(jnp.logical_not(is_mid & mine(m)))
-            def _():
-                onward(m).wait_send()
-
-        loop(0, BLOCKS, drain)
-
+
+        @pl.when(is_mid)
+        def _():
+            sent(rout, BLOCKS // 2, rs_send)
+            for way in range(3):
+                sent(res, BLOCKS // 2, ag_send.at[way])
+
+        @pl.when(jnp.logical_not(is_mid))
+        def _():
+            sent(rout, BLOCKS, rs_send)
+
+    for i in range(3):
+        for copy in along_x(i):
+            copy.wait_send()
     for half in range(2):
-        for copy in along_x(half) + along_y(half):
+        for copy in along_y(half):
             copy.wait_send()
     last.wait()
     dx_ref[...] = (sz[0] + rz[...])[:ROWS].astype(BF16)
@@ -448,7 +472,7 @@
     pick = np.zeros((HALF, HALF // ROWS * SLOT), np.float32)
     pick[row, row // ROWS * SLOT + row % ROWS] = 1.0
     vmem = pl.BlockSpec(memory_space=pltpu.VMEM)
-    hbm = pl.BlockSpec(memory_space=pl.ANY)
+    hbm = pl.BlockSpec(memory_space=pltpu.HBM)
     slots = (2, NY, NX, 2, SLOT, depth)
     wide = (3, TOKENS, width)
     dma = pltpu.SemaphoreType.DMA
@@ -488,13 +512,13 @@
             dma((2, 2, 2, NX - 1)),
             dma((2, 2, NX)),
             dma((2, 2, NX)),
-            dma((2, 2, 2)),
-            dma((BLOCKS,)),
-            dma((BLOCKS,)),
-            dma((BLOCKS,)),
-            dma((3, BLOCKS)),
-            dma((BLOCKS,)),
-            dma((2, 2, NX - 1)),
+            dma((2, 2)),
+            dma,
+            dma((BLOCKS, MATRICES)),
+            dma((BLOCKS, MATRICES)),
+            dma((3,)),
+            dma((BLOCKS, MATRICES)),
+            dma((3, 2, NX - 1)),
             dma((2, 2, NY - 1)),
             dma((2,)),
         ],

time: 99.3 us -> 96.2 us (0.969)
  Pallas kernels: 91.6 us -> 88.7 us
    pallas_call x1, Pallas kernels: 91.6 us -> 88.7 us  [local(): pl.pallas_call(kernel, out_shape=(jax.ShapeDtypeStruct(inputs.shape, BF16...]
where the time goes in v3:
time: 96.2 us; the launch traced here: 95.7 us
  Pallas kernels  88.7 us (92%)
  local copies, waits for them, and re-layouts  6.29 us (7%)
    pallas_call x1, Pallas kernels, local(): pl.pallas_call(kernel, out_shape=(jax.ShapeDtypeStruct(inputs.shape, BF16...  88.7 us
    unnamed x12, local copies, waits for them, and re-layouts  5.54 us

profile of v3, /device:TPU:6, one launch (start us, length us, event | category | flops | bytes accessed | tf_op | source)
XLA Modules:
  0.0 95.7 jit_solution(8522525604563443839)
XLA Ops:
  0.6 0.0 copy-start
  0.6 0.7 copy.12.conf_ref
  1.4 0.0 copy-done
  1.4 0.0 copy-start.1
  1.4 0.7 copy-done.1
  2.1 0.0 copy-start.2
  2.1 0.9 copy-done.2
  3.0 0.0 copy-start.3
  3.0 0.9 copy-done.3
  3.9 88.7 %shard_map.111 = (bf16[12,320]{1,0:T(8,128)(2,1)S(1)}, bf16[320,864]{1,0:T(8,128)(2,1)S(1)}, bf16[320,864]{1,0:T(8,128)(2,1)S(1)}, bf16[320,864]{1,0:T(8,128)(2,1)S(1)}) custom-call(bf16[12,320]{1,0:T(8,128)(2,1)S(1)} %copy-done, bf16[12,320]{1,0:T(8,128)(2,1)S(1)} %copy-done.1, s32[12,1]{1,0:T(8,128)S(1)} %copy.12.conf_ref, bf16[320,864]{1,0:T(8,128)(2,1)} %wg_hbm.1, ...), custom_call_target="tpu_custom_call" | custom-call | flops 2335703040 | bytes 3317760 | tf_op jit(solution)/shard_map/pallas_call | solution.py:479
  92.6 0.6 copy.17
  93.2 0.8 copy.18
  94.0 0.8 copy.19
  94.9 0.8 copy.20
Async XLA Ops:
  0.6 0.8 copy-start
  1.4 0.7 copy-start.1
  2.1 0.9 copy-start.2
  3.0 0.9 copy-start.3

commit v4 on v3

--- a/solution.py
+++ b/solution.py
@@ -1,6 +1,5 @@
 import jax
 import jax.numpy as jnp
-import numpy as np
 from jax import lax
 from jax.experimental import pallas as pl
 from jax.experimental.pallas import tpu as pltpu
@@ -16,9 +15,8 @@
 HALF = TOKENS // 2
 BLOCK = 16
 BLOCKS = TOKENS // BLOCK
-PAIRS = BLOCKS // 2
-CUTS = (0, PAIRS // 4, 3 * PAIRS // 4, PAIRS)
-LEAD = 2
+CUTS = (0, BLOCKS // 4, 3 * BLOCKS // 4, BLOCKS)
+LAG = 4
 MATRICES = 3
 MESH = pl.DeviceIdType.MESH
 
@@ -38,9 +36,9 @@
 
 
 def kernel(
-    x_ref, og_ref, conf_ref, wg_hbm, wu_hbm, wd_hbm, pick_ref, drop_ref,
+    x_ref, og_ref, conf_ref, wg_hbm, wu_hbm, wd_hbm,
     dx_ref, dg_ref, du_ref, dd_ref,
-    xb, sb, xg, sg, xc, sc, w, part, rin, rout, crs, res,
+    pick_ref, drop_ref, xb, sb, xg, sg, xc, sc, w, part, rin, rout, crs, res,
     gxp, rx, sy, ry, sz, rz,
     l_sem, w_sem, own_sem, z_sem, g1_sem, g2_sem, g3_sem, c_sem,
     rs_send, rs_recv, cross_recv, ag_send, ag_recv, x1_sem, x2_sem, x3_sem,
@@ -62,6 +60,7 @@
         )
 
     across = at_dp(y, x, 1 - h, core)
+    across_other = at_dp(y, x, 1 - h, 1 - core)
     x_peers = [at_dp(y, (x + k) % NX, h, core) for k in range(1, NX)]
     y_peers = [at_dp((y + k) % NY, x, h, core) for k in range(1, NY)]
     x_others = [at_dp(y, (x + k) % NX, h, 1 - core) for k in range(1, NX)]
@@ -73,7 +72,7 @@
     def greet(device):
         pl.semaphore_signal(barrier, inc=1, device_id=device, device_id_type=MESH)
 
-    greeted = [across, sibling] + x_peers + y_peers + x_others + y_others
+    greeted = [across, across_other, sibling] + x_peers + y_peers + x_others + y_others
     for device in greeted:
         greet(device)
 
@@ -94,12 +93,20 @@
     for copy in loads:
         copy.start()
 
-    factor = conf_ref[...].astype(F32) / 256.0
+    place = [lax.broadcasted_iota(jnp.int32, (ROWS, ROWS), i) for i in range(2)]
+    spread = jnp.where(place[0] == place[1], conf_ref[...].astype(F32) / 256.0, 0.0)
+    factor = jnp.sum(spread, axis=1, keepdims=True)
     xb[...] = jnp.zeros_like(xb)
     sb[...] = jnp.zeros_like(sb)
     xb[pl.ds(0, ROWS)] = x_ref[...]
     sb[pl.ds(0, ROWS)] = (og_ref[...].astype(F32) * factor).astype(BF16)
 
+    for ref, dim in ((pick_ref, 0), (drop_ref, 1)):
+        dense = lax.broadcasted_iota(jnp.int32, ref.shape, dim).astype(F32)
+        padded = lax.broadcasted_iota(jnp.int32, ref.shape, 1 - dim).astype(F32)
+        slot = jnp.floor((dense + 0.5) / ROWS)
+        ref[...] = jnp.where(padded == dense + slot * (SLOT - ROWS), 1.0, 0.0).astype(BF16)
+
     @pl.when(core == 1)
     def _():
         xg[0, y, x, 1] = xb[...]
@@ -117,17 +124,20 @@
     inner = jnp.where(z <= LEFT, z + 1, z - 1)
     is_end = (z == 0) | (z == LINE - 1)
     is_mid = (z == LEFT) | (z == RIGHT)
-    left_side = jnp.where(z <= LEFT, 1, 0)
 
     own = [
         remote(src, dst.at[0, y, x, 0], own_sem.at[0, i], own_sem.at[1, i], sibling)
         for i, (src, dst) in enumerate(((xb, xg), (sb, sg)))
     ]
     weights = remote(w.at[0], w.at[1], w_sem.at[0], w_sem.at[1], sibling)
-    exchange = [
-        remote(ref.at[0, y, x], ref.at[1, y, x], z_sem.at[0, i], z_sem.at[1, i], across)
-        for i, ref in enumerate((xg, sg))
-    ]
+
+    def exchange(side, target):
+        return [
+            remote(
+                src, dst.at[1, y, x, side], z_sem.at[0, i, side], z_sem.at[1, i, side], target
+            )
+            for i, (src, dst) in enumerate(((xb, xg), (sb, sg)))
+        ]
 
     def gather_first(half):
         copies = []
@@ -167,15 +177,12 @@
     ]
 
     def segment(i):
-        start, stop = CUTS[i] * 2 * BLOCK, CUTS[i + 1] * 2 * BLOCK
+        start, stop = CUTS[i] * BLOCK, CUTS[i + 1] * BLOCK
         slots = (pl.ds(0, NY // 2), pl.ds(0, NY), pl.ds(NY // 2, NY // 2))[i]
         return pl.ds(start, stop - start), i % 2, slots, stop - start
 
     def rows_of(m):
         return pl.ds(pl.multiple_of(m * BLOCK, BLOCK), BLOCK)
-
-    def mine(m):
-        return (m % 2) == (z - LEFT)
 
     def onward(m, i):
         return remote(
@@ -193,9 +200,8 @@
         here = res.at[i, rows_of(m)]
         return remote(here, here, ag_send.at[way], ag_recv.at[m, i], device)
 
-    def sent(buffer, blocks, sem):
-        rows = buffer.at[:, pl.ds(0, blocks * BLOCK)]
-        remote(rows, rows, sem, sem, sibling).wait_send()
+    def sent(buffer, sem):
+        remote(buffer, buffer, sem, sem, sibling).wait_send()
 
     def along_x(i):
         _, half, slots, _ = segment(i)
@@ -251,9 +257,11 @@
 
     @pl.when(core == 1)
     def _():
+        for copy in exchange(1, across):
+            copy.start()
         for copy in own:
             copy.wait_recv()
-        for copy in gather_first(0) + exchange:
+        for copy in gather_first(0):
             copy.start()
         for copy in loads:
             copy.wait()
@@ -262,8 +270,9 @@
             copy.wait_recv()
         for copy in gather_last(0):
             copy.start()
-        for copy in exchange:
-            copy.wait_recv()
+        for side in range(2):
+            for copy in exchange(side, across):
+                copy.wait_recv()
         for copy in gather_first(1):
             copy.start()
         for copy in gather_first(1):
@@ -275,7 +284,7 @@
             for i in range(MATRICES):
                 result(m, i, 0, sibling).wait_recv()
 
-                @pl.when(jnp.logical_not(is_mid & mine(m)))
+                @pl.when(jnp.logical_not(is_mid))
                 def _():
                     result(m, i, 0, sibling).start()
 
@@ -283,36 +292,26 @@
                     def _():
                         result(m, i, 1, at_line(outer, 1)).start()
 
-        def step(s):
-            @pl.when(s < PAIRS)
-            def _():
-                forward(2 * s + 1 - left_side)
-
-            @pl.when(s >= LEAD)
-            def _():
-                forward(2 * (s - LEAD) + left_side)
-
-        loop(0, CUTS[1] + LEAD, step)
+        loop(CUTS[0], CUTS[1], forward)
         back(0)
-        loop(CUTS[1] + LEAD, CUTS[2] + LEAD, step)
+        loop(CUTS[1], CUTS[2], forward)
         back(1)
-        loop(CUTS[2] + LEAD, PAIRS, step)
+        loop(CUTS[2], CUTS[3] - 2, forward)
         sum_x(1)
-        loop(PAIRS, PAIRS + LEAD, step)
+        loop(CUTS[3] - 2, CUTS[3], forward)
         back(2)
         for copy in columns:
             copy.wait_recv()
 
     @pl.when(core == 0)
     def _():
-        for copy in own:
+        for copy in own + exchange(0, across_other):
             copy.start()
 
         def finish(m):
             rows = rows_of(m)
             totals = []
             for i in range(MATRICES):
-                onward(m, i).wait_recv()
                 cross(m, i).wait_recv()
                 totals.append(
                     part[i, rows] + rin[i, rows].astype(F32) + crs[i, rows].astype(F32)
@@ -324,8 +323,7 @@
             for i, value in enumerate((swish * up_pre, gate_grad, back_grad * swish)):
                 res[i, rows] = value.astype(BF16)
                 result(m, i, 0, at_line(outer, 1)).start()
-                result(m, i, 1, at_line(inner, 1)).start()
-                result(m, i, 2, sibling).start()
+                result(m, i, 1, sibling).start()
 
         def add(m):
             rows = rows_of(m)
@@ -368,24 +366,22 @@
                 )
 
         def stream(first, last):
-            def step(s):
-                @pl.when(s < last)
-                def _():
-                    add(2 * s + left_side)
-
-                @pl.when(s >= first + LEAD)
-                def _():
-                    m = 2 * (s - LEAD) + 1 - left_side
-
-                    @pl.when(is_mid)
-                    def _():
-                        finish(m)
-
-                    @pl.when(jnp.logical_not(is_mid))
+            @pl.when(jnp.logical_not(is_mid))
+            def _():
+                loop(first, last, add)
+
+            @pl.when(is_mid)
+            def _():
+                def step(m):
+                    @pl.when(m < last)
                     def _():
                         add(m)
 
-            loop(first, last + LEAD, step)
+                    @pl.when(m >= first + LAG)
+                    def _():
+                        finish(m - LAG)
+
+                loop(first, last + LAG, step)
 
         for copy in gather_last(0):
             copy.wait_recv()
@@ -400,13 +396,15 @@
             copy.start()
 
         def take(m):
-            @pl.when(jnp.logical_not(is_mid & mine(m)))
+            for i in range(MATRICES):
+                result(m, i, 0, sibling).wait_recv()
+
+        for i in range(3):
+
+            @pl.when(jnp.logical_not(is_mid))
             def _():
-                for i in range(MATRICES):
-                    result(m, i, 0, sibling).wait_recv()
-
-        for i in range(3):
-            loop(2 * CUTS[i], 2 * CUTS[i + 1], take)
+                loop(CUTS[i], CUTS[i + 1], take)
+
             back(i)
             if i == 1:
                 sum_x(1)
@@ -422,39 +420,30 @@
 
     @pl.when(core == 1)
     def _():
-        for copy in exchange + [weights]:
+        for copy in exchange(1, across) + [weights]:
             copy.wait_send()
         for half in range(2):
             for copy in gather_first(half) + gather_last(half):
                 copy.wait_send()
 
+        @pl.when(jnp.logical_not(is_mid))
+        def _():
+            sent(res, ag_send.at[0])
+
+            @pl.when(jnp.logical_not(is_end))
+            def _():
+                sent(res, ag_send.at[1])
+
+    @pl.when(core == 0)
+    def _():
+        for copy in own + exchange(0, across_other) + columns:
+            copy.wait_send()
+        sent(rout, rs_send)
+
         @pl.when(is_mid)
         def _():
-            sent(res, BLOCKS // 2, ag_send.at[0])
-            sent(res, BLOCKS // 2, ag_send.at[1])
-
-        @pl.when(jnp.logical_not(is_mid))
-        def _():
-            sent(res, BLOCKS, ag_send.at[0])
-
-            @pl.when(jnp.logical_not(is_end))
-            def _():
-                sent(res, BLOCKS, ag_send.at[1])
-
-    @pl.when(core == 0)
-    def _():
-        for copy in own + columns:
-            copy.wait_send()
-
-        @pl.when(is_mid)
-        def _():
-            sent(rout, BLOCKS // 2, rs_send)
-            for way in range(3):
-                sent(res, BLOCKS // 2, ag_send.at[way])
-
-        @pl.when(jnp.logical_not(is_mid))
-        def _():
-            sent(rout, BLOCKS, rs_send)
+            for way in range(2):
+                sent(res, ag_send.at[way])
 
     for i in range(3):
         for copy in along_x(i):
@@ -468,9 +457,6 @@
 
 def local(inputs, w_gate, w_up, w_down, out_grad, confidence):
     depth, width = w_gate.shape
-    row = np.arange(HALF)
-    pick = np.zeros((HALF, HALF // ROWS * SLOT), np.float32)
-    pick[row, row // ROWS * SLOT + row % ROWS] = 1.0
     vmem = pl.BlockSpec(memory_space=pltpu.VMEM)
     hbm = pl.BlockSpec(memory_space=pltpu.HBM)
     slots = (2, NY, NX, 2, SLOT, depth)
@@ -484,9 +470,11 @@
             jax.ShapeDtypeStruct(w_up.shape, BF16),
             jax.ShapeDtypeStruct((depth, width), BF16),
         ),
-        in_specs=[vmem] * 3 + [hbm] * 3 + [vmem] * 2,
+        in_specs=[vmem] * 3 + [hbm] * 3,
         out_specs=(vmem,) * 4,
         scratch_shapes=[
+            pltpu.VMEM((HALF, HALF // ROWS * SLOT), BF16),
+            pltpu.VMEM((HALF // ROWS * SLOT, HALF), BF16),
             pltpu.VMEM((SLOT, depth), BF16),
             pltpu.VMEM((SLOT, depth), BF16),
             pltpu.VMEM(slots, BF16),
@@ -508,7 +496,7 @@
             dma((3,)),
             dma((2,)),
             dma((2, 2)),
-            dma((2, 2)),
+            dma((2, 2, 2)),
             dma((2, 2, 2, NX - 1)),
             dma((2, 2, NX)),
             dma((2, 2, NX)),
@@ -516,7 +504,7 @@
             dma,
             dma((BLOCKS, MATRICES)),
             dma((BLOCKS, MATRICES)),
-            dma((3,)),
+            dma((2,)),
             dma((BLOCKS, MATRICES)),
             dma((3, 2, NX - 1)),
             dma((2, 2, NY - 1)),
@@ -533,12 +521,10 @@
     )(
         inputs,
         out_grad,
-        confidence[:, None],
+        confidence[None, :],
         w_gate,
         w_up,
         w_down.T,
-        jnp.asarray(pick, BF16),
-        jnp.asarray(pick.T, BF16),
     )
     return grad_x, grad_gate, grad_up, grad_down.T
 

time: 96.2 us -> 93.1 us (0.968)
  Pallas kernels: 88.7 us -> 86.6 us
  local copies, waits for them, and re-layouts: 6.29 us -> 5.09 us
    pallas_call x1, Pallas kernels: 88.7 us -> 86.6 us  [local(): pl.pallas_call(kernel, out_shape=(jax.ShapeDtypeStruct(inputs.shape, BF16...]
    unnamed x12 -> x10, local copies, waits for them, and re-layouts: 5.54 us -> 5.09 us
where the time goes in v4:
time: 93.1 us; the launch traced here: 92.4 us
  Pallas kernels  86.6 us (93%)
  local copies, waits for them, and re-layouts  5.09 us (5%)
    pallas_call x1, Pallas kernels, local(): pl.pallas_call(kernel, out_shape=(jax.ShapeDtypeStruct(inputs.shape, BF16...  86.6 us
    unnamed x10, local copies, waits for them, and re-layouts  5.09 us

profile of v4, /device:TPU:6, one launch (start us, length us, event | category | flops | bytes accessed | tf_op | source)
XLA Modules:
  0.0 92.4 jit_solution(4535471272038296992)
XLA Ops:
  0.6 0.0 copy-start.2
  0.6 0.6 copy-done.2
  1.3 0.0 copy-start
  1.3 0.7 copy-done
  2.0 0.0 copy-start.1
  2.0 0.7 copy-done.1
  2.7 86.6 %shard_map.93 = (bf16[12,320]{1,0:T(8,128)(2,1)S(1)}, bf16[320,864]{1,0:T(8,128)(2,1)S(1)}, bf16[320,864]{1,0:T(8,128)(2,1)S(1)}, bf16[320,864]{1,0:T(8,128)(2,1)S(1)}) custom-call(bf16[12,320]{1,0:T(8,128)(2,1)S(1)} %copy-done, bf16[12,320]{1,0:T(8,128)(2,1)S(1)} %copy-done.1, s32[1,12]{1,0:T(1,128)S(1)} %bitcast.4, bf16[320,864]{1,0:T(8,128)(2,1)} %wg_hbm.1, ...), custom_call_target="tpu_custom_call" | custom-call | flops 2335703040 | bytes 3317760 | tf_op jit(solution)/shard_map/pallas_call | solution.py:465
  89.3 0.6 copy.14
  89.9 0.8 copy.15
  90.7 0.8 copy.16
  91.5 0.8 copy.17
Async XLA Ops:
  0.6 0.7 copy-start.2
  1.3 0.7 copy-start
  2.0 0.7 copy-start.1

commit v5 on v4

--- a/solution.py
+++ b/solution.py
@@ -296,10 +296,9 @@
         back(0)
         loop(CUTS[1], CUTS[2], forward)
         back(1)
-        loop(CUTS[2], CUTS[3] - 2, forward)
+        loop(CUTS[2], CUTS[3], forward)
+        back(2)
         sum_x(1)
-        loop(CUTS[3] - 2, CUTS[3], forward)
-        back(2)
         for copy in columns:
             copy.wait_recv()
 

time: 93.1 us -> 93.9 us (level); the launches traced: 92.4 us -> 92.1 us
  no operation moved by 1% of the time
where the time goes in v5:
time: 93.9 us; the launch traced here: 92.1 us
  Pallas kernels  86.4 us (92%)
  local copies, waits for them, and re-layouts  5.09 us (5%)
    pallas_call x1, Pallas kernels, local(): pl.pallas_call(kernel, out_shape=(jax.ShapeDtypeStruct(inputs.shape, BF16...  86.4 us
    unnamed x10, local copies, waits for them, and re-layouts  5.09 us

profile of v5, /device:TPU:6, one launch (start us, length us, event | category | flops | bytes accessed | tf_op | source)
XLA Modules:
  0.0 92.1 jit_solution(8666251870872332630)
XLA Ops:
  0.6 0.0 copy-start.2
  0.6 0.6 copy-done.2
  1.3 0.0 copy-start
  1.3 0.7 copy-done
  2.0 0.0 copy-start.1
  2.0 0.7 copy-done.1
  2.7 86.4 %shard_map.93 = (bf16[12,320]{1,0:T(8,128)(2,1)S(1)}, bf16[320,864]{1,0:T(8,128)(2,1)S(1)}, bf16[320,864]{1,0:T(8,128)(2,1)S(1)}, bf16[320,864]{1,0:T(8,128)(2,1)S(1)}) custom-call(bf16[12,320]{1,0:T(8,128)(2,1)S(1)} %copy-done, bf16[12,320]{1,0:T(8,128)(2,1)S(1)} %copy-done.1, s32[1,12]{1,0:T(1,128)S(1)} %bitcast.4, bf16[320,864]{1,0:T(8,128)(2,1)} %wg_hbm.1, ...), custom_call_target="tpu_custom_call" | custom-call | flops 2335703040 | bytes 3317760 | tf_op jit(solution)/shard_map/pallas_call | solution.py:464
  89.1 0.6 copy.14
  89.7 0.8 copy.15
  90.5 0.8 copy.16
  91.3 0.8 copy.17
Async XLA Ops:
  0.6 0.7 copy-start.2
  1.3 0.7 copy-start
  2.0 0.7 copy-start.1

commit v6 on v4

--- a/solution.py
+++ b/solution.py
@@ -15,7 +15,7 @@
 HALF = TOKENS // 2
 BLOCK = 16
 BLOCKS = TOKENS // BLOCK
-CUTS = (0, BLOCKS // 4, 3 * BLOCKS // 4, BLOCKS)
+CUTS = (0, BLOCKS // 8, 5 * BLOCKS // 8, BLOCKS)
 LAG = 4
 MATRICES = 3
 MESH = pl.DeviceIdType.MESH
@@ -178,7 +178,7 @@
 
     def segment(i):
         start, stop = CUTS[i] * BLOCK, CUTS[i + 1] * BLOCK
-        slots = (pl.ds(0, NY // 2), pl.ds(0, NY), pl.ds(NY // 2, NY // 2))[i]
+        slots = (pl.ds(0, 1), pl.ds(0, NY), pl.ds(1, NY - 1))[i]
         return pl.ds(start, stop - start), i % 2, slots, stop - start
 
     def rows_of(m):
@@ -255,6 +255,8 @@
             total = total + ry[half, k]
         sz[half] = total
 
+    last = remote(sz.at[1], rz, x3_sem.at[0], x3_sem.at[1], across)
+
     @pl.when(core == 1)
     def _():
         for copy in exchange(1, across):
@@ -296,9 +298,12 @@
         back(0)
         loop(CUTS[1], CUTS[2], forward)
         back(1)
-        loop(CUTS[2], CUTS[3] - 2, forward)
+        loop(CUTS[2], CUTS[3] - 5, forward)
         sum_x(1)
-        loop(CUTS[3] - 2, CUTS[3], forward)
+        loop(CUTS[3] - 5, CUTS[3] - 1, forward)
+        sum_y(1)
+        last.start()
+        loop(CUTS[3] - 1, CUTS[3], forward)
         back(2)
         for copy in columns:
             copy.wait_recv()
@@ -405,13 +410,13 @@
             def _():
                 loop(CUTS[i], CUTS[i + 1], take)
 
+            if i == 2:
+                sum_y(1)
+                last.start()
             back(i)
             if i == 1:
                 sum_x(1)
 
-    sum_y(1)
-    last = remote(sz.at[1], rz, x3_sem.at[0], x3_sem.at[1], across)
-    last.start()
     dg_ref[...] = contract(xc[0], res[1], 0, 0).astype(BF16)
     sum_x(0)
     du_ref[...] = contract(xc[0], res[2], 0, 0).astype(BF16)

time: 93.1 us -> 94.4 us (1.014)
  Pallas kernels: 86.6 us -> 87.8 us
    pallas_call x1, Pallas kernels: 86.6 us -> 87.8 us  [local(): pl.pallas_call(kernel, out_shape=(jax.ShapeDtypeStruct(inputs.shape, BF16...]
where the time goes in v6:
time: 94.4 us; the launch traced here: 93.6 us
  Pallas kernels  87.8 us (93%)
  local copies, waits for them, and re-layouts  5.09 us (5%)
    pallas_call x1, Pallas kernels, local(): pl.pallas_call(kernel, out_shape=(jax.ShapeDtypeStruct(inputs.shape, BF16...  87.8 us
    unnamed x10, local copies, waits for them, and re-layouts  5.09 us

profile of v6, /device:TPU:6, one launch (start us, length us, event | category | flops | bytes accessed | tf_op | source)
XLA Modules:
  0.0 93.6 jit_solution(13761837944172297070)
XLA Ops:
  0.6 0.0 copy-start.2
  0.6 0.6 copy-done.2
  1.3 0.0 copy-start
  1.3 0.7 copy-done
  2.0 0.0 copy-start.1
  2.0 0.7 copy-done.1
  2.7 87.8 %shard_map.93 = (bf16[12,320]{1,0:T(8,128)(2,1)S(1)}, bf16[320,864]{1,0:T(8,128)(2,1)S(1)}, bf16[320,864]{1,0:T(8,128)(2,1)S(1)}, bf16[320,864]{1,0:T(8,128)(2,1)S(1)}) custom-call(bf16[12,320]{1,0:T(8,128)(2,1)S(1)} %copy-done, bf16[12,320]{1,0:T(8,128)(2,1)S(1)} %copy-done.1, s32[1,12]{1,0:T(1,128)S(1)} %bitcast.4, bf16[320,864]{1,0:T(8,128)(2,1)} %wg_hbm.1, ...), custom_call_target="tpu_custom_call" | custom-call | flops 2335703040 | bytes 3317760 | tf_op jit(solution)/shard_map/pallas_call | solution.py:470
  90.5 0.6 copy.14
  91.2 0.8 copy.15
  92.0 0.8 copy.16
  92.8 0.8 copy.17
Async XLA Ops:
  0.6 0.7 copy-start.2
  1.3 0.7 copy-start
  2.0 0.7 copy-start.1
